TPU v7x, 32 devices: a whole 2x2x4 slice. The times are simulated.
32 devices in a mesh: unit: 16 (over z, y, x), samp: 2 (over core).
Axes of the slice: x: 2, y: 2, z: 4, core: 2. Of those that a mesh axis runs over, the one named last changes fastest.
Arguments:
- abundance: float32 [16384, 4096], P('unit', 'samp'), may hold values from 0.0009 to 27, as said below
- unitig_factor: float32 [16384, 128], P('unit'), may hold values from 0.005 to 1.8, as said below
- sample_factor: float32 [4096, 128], P('samp'), may hold values from 0.02 to 0.2
Outputs:
- unitig_update: float32 [16384, 128], P('unit')
- sample_update: float32 [4096, 128], P('samp')
Inputs may be any that keep to these rules, and one draw needn't show every extreme that they name: abundance entries are positive. unitig_factor entries are positive.
All inputs are finite; a program needn't handle non-finite values.
Results may differ from a plain program's by a relative error of at most 0.0001.
Values sent between devices are 32-bit elements; how exact they have to be, the bound alone decides.
A program may use at most 64 MiB of HBM per device.

v0:
```python
import jax
import jax.numpy as jnp
from jax import lax
from jax.sharding import PartitionSpec as P

ITERS = 2


HI = lax.Precision.HIGHEST


def inner(left, right):
    return lax.dot_general(
        left, right, (((0,), (0,)), ((), ())), precision=HI, preferred_element_type=jnp.float32
    )


def shards(abundance, unitig_factor, sample_factor):
    unitig = unitig_factor
    sample = sample_factor
    for sweep in range(ITERS):
        target_h, gram_unit = lax.psum((inner(abundance, unitig), inner(unitig, unitig)), "unit")
        sample = sample * target_h / jnp.dot(sample, gram_unit, precision=HI)
        target_w, gram_sample = lax.psum(
            (jnp.dot(abundance, sample, precision=HI), inner(sample, sample)), "samp"
        )
        unitig = unitig * target_w / jnp.dot(unitig, gram_sample, precision=HI)
    return (unitig, sample)


def solution(mesh):
    return jax.shard_map(
        shards,
        mesh=mesh,
        in_specs=(P("unit", "samp"), P("unit", None), P("samp", None)),
        out_specs=(P("unit", None), P("samp", None)),
        check_vma=False,
    )
```

profile of v0, /device:TPU:0, one launch (start us, length us, event | category | flops | bytes accessed | tf_op | source)
XLA Modules:
  0.0 354.7 jit_solution(3777715741044157550)
XLA Ops:
  7.2 0.0 all-reduce.11.cloned.1.call-start
  7.2 2.9 fusion.3
  10.1 0.0 copy-start.2
  10.1 16.5 %fusion.2 = f32[2048,128]{1,0:T(8,128)} fusion(f32[1024,2048]{1,0:T(8,128)} %param.3, f32[1024,128]{1,0:T(8,128)} %param.4), kind=kOutput, calls=%fused_computation.9 | convolution fusion | flops 3221225472 | bytes 9961472 | tf_op jit(solution)/shard_map/dot_general | solution.py:13
  26.6 0.0 all-reduce.11.cloned.1.call-update
  26.6 0.0 copy-start
  26.6 0.2 all-reduce.15.cloned.1.call-start
  26.9 115.6 %all-reduce.11.cloned.1.call-done = (f32[128,128]{1,0:T(8,128)}, f32[2048,128]{1,0:T(8,128)}) async-done(((f32[128,128]{1,0:T(8,128)}, f32[2048,128]{1,0:T(8,128)}), (f32[128,128]{1,0:T(8,128)}, f32[2048,128]{1,0:T(8,128)})) %all-reduce.11.cloned.1.call-update) | async-done | bytes 1114128 | tf_op jit(solution)/shard_map/psum | solution.py:22
  142.5 0.0 copy-done.2
  142.5 2.2 fusion
  144.7 2.5 fusion.4
  147.2 11.9 %convolution_bitcast_fusion.4 = f32[1024,128]{0,1:T(8,128)} fusion(f32[2048,128]{1,0:T(8,128)S(1)} %fusion, f32[1024,2048]{1,0:T(8,128)} %param.3), kind=kOutput, calls=%fused_computation.6 | convolution fusion | flops 3221225472 | bytes 9961472 | tf_op jit(solution)/shard_map/dot_general | solution.py:25
  159.1 0.0 all-reduce.15.cloned.1.call-update
  159.2 0.3 all-reduce.9.cloned.1.call-start
  159.4 0.0 copy-done
  159.4 0.2 copy.6
  159.6 17.5 %all-reduce.15.cloned.1.call-done = (f32[128,128]{1,0:T(8,128)}, f32[1024,128]{0,1:T(8,128)}) async-done(((f32[128,128]{1,0:T(8,128)}, f32[1024,128]{0,1:T(8,128)}), (f32[128,128]{1,0:T(8,128)}, f32[1024,128]{0,1:T(8,128)})) %all-reduce.15.cloned.1.call-update) | async-done | bytes 589840 | tf_op jit(solution)/shard_map/psum | solution.py:24
  177.1 1.8 fusion.1
  178.9 1.2 fusion.5
  180.1 16.3 %convolution_bitcast_fusion = f32[2048,128]{1,0:T(8,128)} fusion(f32[1024,128]{0,1:T(8,128)S(1)} %fusion.1, f32[1024,2048]{1,0:T(8,128)} %param.3), kind=kOutput, calls=%fused_computation | convolution fusion | flops 3221225472 | bytes 9961472 | tf_op jit(solution)/shard_map/dot_general | solution.py:13
  196.4 0.0 all-reduce.9.cloned.1.call-update
  196.4 0.3 all-reduce.13.cloned.1.call-start
  196.7 114.1 %all-reduce.9.cloned.1.call-done = (f32[128,128]{1,0:T(8,128)}, f32[2048,128]{1,0:T(8,128)}) async-done(((f32[128,128]{1,0:T(8,128)}, f32[2048,128]{1,0:T(8,128)}), (f32[128,128]{1,0:T(8,128)}, f32[2048,128]{1,0:T(8,128)})) %all-reduce.9.cloned.1.call-update) | async-done | bytes 1114128 | tf_op jit(solution)/shard_map/psum | solution.py:22
  310.8 2.2 convolution_divide_fusion
  313.1 0.0 copy-start.1
  313.1 2.4 fusion.6
  315.5 11.9 %convolution_bitcast_fusion.2 = f32[1024,128]{0,1:T(8,128)} fusion(f32[2048,128]{1,0:T(8,128)S(1)} %convolution_divide_fusion, f32[1024,2048]{1,0:T(8,128)} %param.3), kind=kOutput, calls=%fused_computation.4 | convolution fusion | flops 3221225472 | bytes 9961472 | tf_op jit(solution)/shard_map/dot_general | solution.py:25
  327.5 0.0 all-reduce.13.cloned.1.call-update
  327.5 17.9 %all-reduce.13.cloned.1.call-done = (f32[128,128]{1,0:T(8,128)}, f32[1024,128]{0,1:T(8,128)}) async-done(((f32[128,128]{1,0:T(8,128)}, f32[1024,128]{0,1:T(8,128)}), (f32[128,128]{1,0:T(8,128)}, f32[1024,128]{0,1:T(8,128)})) %all-reduce.13.cloned.1.call-update) | async-done | bytes 589840 | tf_op jit(solution)/shard_map/psum | solution.py:24
  345.4 1.7 convolution_divide_fusion.1
  347.2 1.0 copy.9
  348.2 0.0 copy-done.1
Async XLA Ops:
  7.2 135.3 %all-reduce.11.cloned.1.call-start = ((), (), s32[]{:S(2)}) async-start(), calls=%async_computation.1 | async-start | bytes 2228224 | tf_op jit(solution)/shard_map/psum | solution.py:22
  10.1 132.4 %copy-start.2 = (f32[2048,128]{1,0:T(8,128)S(1)}, f32[2048,128]{1,0:T(8,128)}, u32[]{:S(2)}) copy-start(f32[2048,128]{1,0:T(8,128)} %param.5) | copy-start | bytes 3145732
  26.6 132.8 %copy-start = (f32[1024,128]{1,0:T(8,128)S(1)}, f32[1024,128]{1,0:T(8,128)}, u32[]{:S(2)}) copy-start(f32[1024,128]{1,0:T(8,128)} %param.4) | copy-start | bytes 1572868
  26.6 150.5 %all-reduce.15.cloned.1.call-start = ((), (), s32[]{:S(2)}) async-start(), calls=%async_computation.3 | async-start | bytes 1179648 | tf_op jit(solution)/shard_map/psum | solution.py:24
  159.2 151.7 %all-reduce.9.cloned.1.call-start = ((), (), s32[]{:S(2)}) async-start(), calls=%async_computation | async-start | bytes 2228224 | tf_op jit(solution)/shard_map/psum | solution.py:22
  196.4 149.0 %all-reduce.13.cloned.1.call-start = ((), (), s32[]{:S(2)}) async-start(), calls=%async_computation.2 | async-start | bytes 1179648 | tf_op jit(solution)/shard_map/psum | solution.py:24
  313.1 35.1 %copy-start.1 = (f32[2048,128]{1,0:T(8,128)}, f32[2048,128]{1,0:T(8,128)S(1)}, u32[]{:S(2)}) copy-start(f32[2048,128]{1,0:T(8,128)S(1)} %convolution_divide_fusion) | copy-start | bytes 3145732
Sparse Core Ops, SparseCore 0:
  26.8 115.6 all-reduce.10
  159.3 17.7 all-reduce.14
  196.6 114.2 all-reduce.8
  327.6 17.7 all-reduce.12
where the time goes:
time: 355 us
  waiting for transfers between devices  265 us (75%)
  matrix products  73.7 us (21%)
  between operations  13.8 us (4%)
    psum x2, waiting for transfers between devices, shards(): lax.psum((inner(abundance, unitig), inner(unitig, unitig)), 'unit')  230 us
    dot_general x6, matrix products, inner(): lax.dot_general(left, right, (((0,), (0,)), ((), ())), precision=HI, pref...  41.8 us
    psum x2, waiting for transfers between devices, shards(): lax.psum((jnp.dot(abundance, sample, precision=HI), inner(sample, sample)...  35.4 us
    dot_general x2, matrix products, shards(): jnp.dot(abundance, sample, precision=HI)  23.9 us
  transfers between devices with their start and end apart: 4, of which 4 were waited for; matrix products, arithmetic and copies ran while one was open for 0% of the time, Pallas kernels for 0%

commit v1 on v0

v1 whole, which is shorter than its diff:
```python
import functools

import jax
import jax.numpy as jnp
from jax import lax
from jax.experimental import pallas as pl
from jax.experimental.pallas import tpu as pltpu
from jax.sharding import PartitionSpec as P

ITERS = 2
PARTS = 4
HI = lax.Precision.HIGHEST
MESH = pl.DeviceIdType.MESH
BF = jnp.bfloat16


def chip_dims(unit):
    n = 1
    while 2 * n * n * n < unit:
        n += 1
    return (n, n, 2 * n) if 2 * n * n * n == unit else (1, 1, unit)


class Plan:
    def __init__(self, unit, samples, rank):
        self.unit = unit
        self.dims = chip_dims(unit)
        x, y, _ = self.dims
        self.strides = (1, x, x * y)
        self.orders = [(0, 1, 2) if p % 2 == 0 else (1, 0, 2) for p in range(PARTS)]
        self.cols = samples // PARTS
        granule = 8 * unit
        self.used = [self.cols + (rank if p == 0 else 0) for p in range(PARTS)]
        self.rows = [-(-used // granule) * granule for used in self.used]
        self.base = [sum(self.rows[:p]) for p in range(PARTS)]
        self.total = sum(self.rows)
        self.slot, self.sem = {}, {}
        rows = sems = 0
        for p in range(PARTS):
            size = self.rows[p]
            for t in range(3):
                n = self.dims[self.orders[p][t]]
                size //= n
                for k in range(1, n):
                    self.slot[p, t, k] = rows
                    self.sem[p, t, k] = sems
                    rows += size
                    sems += 1
        self.recv_rows, self.sems = max(rows, 8), max(sems, 1)


def split(value):
    high = value.astype(BF)
    return high, (value - high.astype(jnp.float32)).astype(BF)


def dot(left, right):
    return jnp.dot(left, right, preferred_element_type=jnp.float32)


def kernel(
    plan, a_hbm, w_in, h_in, w_ref, h_ref,
    a_f32, a_high, a_low, wt, acc, gat, rsr, q_own, q_peer, f_sum,
    load_sem, rs_send, rs_recv, ag_send, ag_recv, q_send, q_recv,
):
    units, rank = w_in.shape
    cols = plan.cols
    me = lax.axis_index("unit")
    core = lax.axis_index("samp")
    place = [lax.rem(me // plan.strides[d], plan.dims[d]) for d in range(3)]
    block = 256

    loads = [
        pltpu.make_async_copy(
            a_hbm.at[:, pl.ds(p * cols, cols)], a_f32.at[p], load_sem.at[p]
        )
        for p in range(PARTS)
    ]
    for load in loads:
        load.start()

    def peer_of(d, k):
        other = lax.rem(place[d] + k, plan.dims[d])
        return other, me + (other - place[d]) * plan.strides[d]

    barrier = pltpu.get_barrier_semaphore()
    greeted = 1
    pl.semaphore_signal(barrier, inc=1, device_id={"samp": 1 - core}, device_id_type=MESH)
    for d in range(3):
        for k in range(1, plan.dims[d]):
            pl.semaphore_signal(
                barrier, inc=1, device_id={"unit": peer_of(d, k)[1]}, device_id_type=MESH
            )
            greeted += 1
    pl.semaphore_wait(barrier, greeted)

    offs, sizes = [], []
    for p in range(PARTS):
        off, size = plan.base[p], plan.rows[p]
        offs.append([off])
        sizes.append([size])
        for t in range(3):
            d = plan.orders[p][t]
            size //= plan.dims[d]
            off = off + place[d] * size
            offs[p].append(off)
            sizes[p].append(size)

    def rows_at(off, size):
        return pl.ds(off if isinstance(off, int) else pl.multiple_of(off, 8), size)

    def rs_copies(it, p, t):
        d, size = plan.orders[p][t], sizes[p][t + 1]
        copies = []
        for k in range(1, plan.dims[d]):
            other, device = peer_of(d, k)
            sem = plan.sem[p, t, k]
            copies.append(pltpu.make_async_remote_copy(
                src_ref=acc.at[it, rows_at(offs[p][t] + other * size, size)],
                dst_ref=rsr.at[it, pl.ds(plan.slot[p, t, k], size)],
                send_sem=rs_send.at[it, sem],
                recv_sem=rs_recv.at[it, sem],
                device_id={"unit": device},
                device_id_type=MESH,
            ))
        return copies

    def ag_copies(it, p, t):
        d, size = plan.orders[p][t], sizes[p][t + 1]
        copies = []
        for k in range(1, plan.dims[d]):
            _, device = peer_of(d, k)
            sem = plan.sem[p, t, k]
            here = gat.at[it, rows_at(offs[p][t + 1], size)]
            copies.append(pltpu.make_async_remote_copy(
                src_ref=here,
                dst_ref=here,
                send_sem=ag_send.at[it, sem],
                recv_sem=ag_recv.at[it, sem],
                device_id={"unit": device},
                device_id_type=MESH,
            ))
        return copies

    def q_copy(it, b, start, size):
        return pltpu.make_async_remote_copy(
            src_ref=q_own.at[it, pl.ds(start, size)],
            dst_ref=q_peer.at[it, pl.ds(start, size)],
            send_sem=q_send.at[it, b],
            recv_sem=q_recv.at[it, b],
            device_id={"samp": 1 - core},
            device_id_type=MESH,
        )

    def start_all(copies):
        for copy in copies:
            copy.start()

    w_ref[...] = w_in[...]
    h_ref[...] = h_in[...]
    turned = w_in[...].T
    wt[:rank], wt[rank:] = split(turned)

    for it in range(ITERS):
        sent = []
        for p in range(PARTS):
            if p == 0:
                acc[it, pl.ds(plan.base[0] + cols, rank)] = jnp.dot(
                    w_ref[...].T, w_ref[...], precision=HI, preferred_element_type=jnp.float32
                )
            if plan.rows[p] > plan.used[p]:
                spare = plan.rows[p] - plan.used[p]
                acc[it, pl.ds(plan.base[p] + plan.used[p], spare)] = jnp.zeros(
                    (spare, rank), jnp.float32
                )
            if it == 0:
                loads[p].wait()
                a_high[p], a_low[p] = split(a_f32[p])
            both = dot(wt[...], a_high[p])
            product = both[:rank] + (both[rank:] + dot(wt[:rank], a_low[p]))
            acc[it, pl.ds(plan.base[p], cols)] = product.T
            copies = rs_copies(it, p, 0)
            start_all(copies)
            sent.append(copies)

        for t in range(3):
            for p in range(PARTS):
                size = sizes[p][t + 1]
                mine = rows_at(offs[p][t + 1], size)
                n = plan.dims[plan.orders[p][t]]
                for copy in sent[p]:
                    copy.wait()
                value = acc[it, mine]
                for k in range(1, n):
                    value = value + rsr[it, pl.ds(plan.slot[p, t, k], size)]
                if t < 2:
                    acc[it, mine] = value
                    sent[p] = rs_copies(it, p, t + 1)
                else:
                    gat[it, mine] = value
                    sent[p] = ag_copies(it, p, 2)
                start_all(sent[p])

        for t in (2, 1, 0):
            for p in range(PARTS):
                for copy in sent[p]:
                    copy.wait()
                if t > 0:
                    sent[p] = ag_copies(it, p, t - 1)
                    start_all(sent[p])
                    continue
                here = pl.ds(p * cols, cols)
                old = h_ref[here]
                gram = gat[it, pl.ds(plan.base[0] + cols, rank)]
                new = old * gat[it, pl.ds(plan.base[p], cols)] / jnp.dot(
                    old, gram, precision=HI, preferred_element_type=jnp.float32
                )
                h_ref[here] = new
                part_f = jnp.dot(
                    new.T, new, precision=HI, preferred_element_type=jnp.float32
                )
                tail = pl.ds(units, rank)
                q_own[it, tail] = part_f if p == 0 else q_own[it, tail] + part_f
                crossing = []
                if p == PARTS - 1:
                    crossing.append(q_copy(it, 0, units, rank))
                    crossing[0].start()
                high, low = split(new)
                pair = jnp.concatenate([high, low], axis=1)
                for b in range(units // block):
                    rows = pl.ds(b * block, block)
                    both = dot(a_high[p, rows], pair)
                    value = both[:, :rank] + (both[:, rank:] + dot(a_low[p, rows], high))
                    q_own[it, rows] = value if p == 0 else q_own[it, rows] + value
                    if p == PARTS - 1:
                        crossing.append(q_copy(it, b + 1, b * block, block))
                        crossing[-1].start()

        crossing[0].wait()
        f_sum[...] = q_own[it, pl.ds(units, rank)] + q_peer[it, pl.ds(units, rank)]
        for b in range(units // block):
            rows = pl.ds(b * block, block)
            crossing[b + 1].wait()
            old = w_ref[rows]
            new = old * (q_own[it, rows] + q_peer[it, rows]) / jnp.dot(
                old, f_sum[...], precision=HI, preferred_element_type=jnp.float32
            )
            w_ref[rows] = new
            if it < ITERS - 1:
                wt[:rank, rows], wt[rank:, rows] = split(new.T)


def shards(unit, abundance, unitig_factor, sample_factor):
    units, samples = abundance.shape
    rank = unitig_factor.shape[1]
    plan = Plan(unit, samples, rank)
    cols = plan.cols
    f32 = jnp.float32
    vmem = pl.BlockSpec(memory_space=pltpu.VMEM)
    blocks = units // 256 + 1
    flops = 4 * 3 * 2 * units * samples * rank
    return pl.pallas_call(
        functools.partial(kernel, plan),
        out_shape=(
            jax.ShapeDtypeStruct((units, rank), f32),
            jax.ShapeDtypeStruct((samples, rank), f32),
        ),
        in_specs=[pl.BlockSpec(memory_space=pl.ANY), vmem, vmem],
        out_specs=(vmem, vmem),
        scratch_shapes=[
            pltpu.VMEM((PARTS, units, cols), f32),
            pltpu.VMEM((PARTS, units, cols), BF),
            pltpu.VMEM((PARTS, units, cols), BF),
            pltpu.VMEM((2 * rank, units), BF),
            pltpu.VMEM((ITERS, plan.total, rank), f32),
            pltpu.VMEM((ITERS, plan.total, rank), f32),
            pltpu.VMEM((ITERS, plan.recv_rows, rank), f32),
            pltpu.VMEM((ITERS, units + rank, rank), f32),
            pltpu.VMEM((ITERS, units + rank, rank), f32),
            pltpu.VMEM((rank, rank), f32),
            pltpu.SemaphoreType.DMA((PARTS,)),
            pltpu.SemaphoreType.DMA((ITERS, plan.sems)),
            pltpu.SemaphoreType.DMA((ITERS, plan.sems)),
            pltpu.SemaphoreType.DMA((ITERS, plan.sems)),
            pltpu.SemaphoreType.DMA((ITERS, plan.sems)),
            pltpu.SemaphoreType.DMA((ITERS, blocks)),
            pltpu.SemaphoreType.DMA((ITERS, blocks)),
        ],
        compiler_params=pltpu.CompilerParams(
            collective_id=0, has_side_effects=True, vmem_limit_bytes=56 * 2**20
        ),
        cost_estimate=pl.CostEstimate(
            flops=flops, bytes_accessed=4 * units * samples, transcendentals=0
        ),
    )(abundance, unitig_factor, sample_factor)


def solution(mesh):
    return jax.shard_map(
        functools.partial(shards, mesh.shape["unit"]),
        mesh=mesh,
        in_specs=(P("unit", "samp"), P("unit", None), P("samp", None)),
        out_specs=(P("unit", None), P("samp", None)),
        check_vma=False,
    )
```

time: 355 us -> 95 us (0.27)
  waiting for transfers between devices: 265 us -> 0 us
  Pallas kernels: 0 us -> 90 us
  matrix products: 73.7 us -> 0 us
  between operations: 13.8 us -> 0.64 us
    psum x4 -> x0, waiting for transfers between devices: 265 us -> none  [the longest x2 230 us: shards(): lax.psum((inner(abundance, unitig), inner(unitig, unitig)), 'unit')]
    pallas_call x0 -> x1, Pallas kernels: none -> 90 us  [shards(): pl.pallas_call(functools.partial(kernel, plan), out_shape=(jax.ShapeDtype...]
    dot_general x12 -> x0, matrix products: 73.7 us -> none  [the longest x6 41.8 us: inner(): lax.dot_general(left, right, (((0,), (0,)), ((), ())), precision=HI, pref...]
  transfers between devices with their start and end apart: 4 -> 0, of which waited for: 4 -> 0; matrix products, arithmetic and copies ran while one was open for 0% -> 0% of each run, Pallas kernels for 0% -> 0%
where the time goes in v1:
time: 95 us; the launch traced here: 94.7 us
  Pallas kernels  90 us (95%)
  local copies, waits for them, and re-layouts  4.13 us (4%)
    pallas_call x1, Pallas kernels, shards(): pl.pallas_call(functools.partial(kernel, plan), out_shape=(jax.ShapeDtype...  90 us
    unnamed x2, local copies, waits for them, and re-layouts  4.13 us

profile of v1, /device:TPU:0, one launch (start us, length us, event | category | flops | bytes accessed | tf_op | source)
XLA Modules:
  0.0 94.7 jit_solution(10425559803523977724)
XLA Ops:
  0.6 90.0 %shard_map.50 = (f32[1024,128]{1,0:T(8,128)}, f32[2048,128]{1,0:T(8,128)}) custom-call(f32[1024,2048]{1,0:T(8,128)} %a_hbm.1, f32[1024,128]{1,0:T(8,128)} %w_in.1, f32[2048,128]{1,0:T(8,128)} %h_in.1), custom_call_target="tpu_custom_call" | custom-call | flops 6442450944 | bytes 8388608 | tf_op jit(solution)/shard_map/pallas_call | solution.py:262
  90.6 1.9 %copy.7 = f32[1024,128]{1,0:T(8,128)} copy(f32[1024,128]{1,0:T(8,128)} %get-tuple-element.4) | data formatting | bytes 1048576
  92.5 2.3 %copy.8 = f32[2048,128]{1,0:T(8,128)} copy(f32[2048,128]{1,0:T(8,128)} %get-tuple-element.5) | data formatting | bytes 2097152

commit v2 on v1

--- a/solution.py
+++ b/solution.py
@@ -9,7 +9,6 @@
 
 ITERS = 2
 PARTS = 4
-HI = lax.Precision.HIGHEST
 MESH = pl.DeviceIdType.MESH
 BF = jnp.bfloat16
 
@@ -58,10 +57,42 @@
     return jnp.dot(left, right, preferred_element_type=jnp.float32)
 
 
+def pack(square):
+    high, low = split(square)
+    return jnp.concatenate(
+        [
+            jnp.concatenate([high, low], axis=1),
+            jnp.concatenate([high, jnp.zeros_like(high)], axis=1),
+        ],
+        axis=0,
+    )
+
+
+def dot_packed(left, packed):
+    rank = left.shape[1]
+    both = dot(jnp.concatenate(split(left), axis=1), packed)
+    return both[:, :rank] + both[:, rank:]
+
+
+def gram_of(turned, pair):
+    rank = turned.shape[0] // 2
+    four = dot(turned, pair)
+    return four[:rank, :rank] + (
+        four[rank:, :rank] + four[:rank, rank:] + four[rank:, rank:]
+    )
+
+
+EVENTS = (
+    (0, 0), (1, 0), (0, 1), (1, 1), (2, 0), (3, 0), (0, 2), (1, 2), (2, 1), (3, 1),
+    (0, 3), (1, 3), (2, 2), (3, 2), (0, 4), (1, 4), (0, 5), (2, 3), (3, 3), (1, 5),
+    (2, 4), (3, 4), (2, 5), (3, 5),
+)
+
+
 def kernel(
-    plan, a_hbm, w_in, h_in, w_ref, h_ref,
-    a_f32, a_high, a_low, wt, acc, gat, rsr, q_own, q_peer, f_sum,
-    load_sem, rs_send, rs_recv, ag_send, ag_recv, q_send, q_recv,
+    plan, a_hbm, w_in, h_in, w_ref, h_out,
+    a_f32, a_high, a_low, wt, acc, gat, rsr, q_own, q_peer, g_pack, f_pack, h_ref,
+    load_sem, h_sem, rs_send, rs_recv, ag_send, ag_recv, q_send, q_recv,
 ):
     units, rank = w_in.shape
     cols = plan.cols
@@ -78,6 +109,8 @@
     ]
     for load in loads:
         load.start()
+    h_load = pltpu.make_async_copy(h_in, h_ref, h_sem)
+    h_load.start()
 
     def peer_of(d, k):
         other = lax.rem(place[d] + k, plan.dims[d])
@@ -92,8 +125,6 @@
                 barrier, inc=1, device_id={"unit": peer_of(d, k)[1]}, device_id_type=MESH
             )
             greeted += 1
-    pl.semaphore_wait(barrier, greeted)
-
     offs, sizes = [], []
     for p in range(PARTS):
         off, size = plan.base[p], plan.rows[p]
@@ -156,98 +187,120 @@
         for copy in copies:
             copy.start()
 
+    def products(it, p, sent):
+        if p == 0:
+            acc[it, pl.ds(plan.base[0] + cols, rank)] = gram_of(
+                wt[...], jnp.concatenate(split(w_ref[...]), axis=1)
+            )
+        if plan.rows[p] > plan.used[p]:
+            spare = plan.rows[p] - plan.used[p]
+            acc[it, pl.ds(plan.base[p] + plan.used[p], spare)] = jnp.zeros(
+                (spare, rank), jnp.float32
+            )
+        if it == 0:
+            loads[p].wait()
+            a_high[p], a_low[p] = split(a_f32[p])
+        both = dot(wt[...], a_high[p])
+        product = both[:rank] + (both[rank:] + dot(wt[:rank], a_low[p]))
+        acc[it, pl.ds(plan.base[p], cols)] = product.T
+        if it == 0 and p == 0:
+            pl.semaphore_wait(barrier, greeted)
+        sent[p] = rs_copies(it, p, 0)
+        start_all(sent[p])
+
+    def advance(it, p, stage, sent):
+        for copy in sent[p]:
+            copy.wait()
+        if stage < 3:
+            size = sizes[p][stage + 1]
+            mine = rows_at(offs[p][stage + 1], size)
+            value = acc[it, mine]
+            for k in range(1, plan.dims[plan.orders[p][stage]]):
+                value = value + rsr[it, pl.ds(plan.slot[p, stage, k], size)]
+            if stage < 2:
+                acc[it, mine] = value
+                sent[p] = rs_copies(it, p, stage + 1)
+            else:
+                gat[it, mine] = value
+                sent[p] = ag_copies(it, p, 2)
+            start_all(sent[p])
+        elif stage < 5:
+            sent[p] = ag_copies(it, p, 4 - stage)
+            start_all(sent[p])
+
+    def update_sample(it, p, h_store):
+        if p == 0:
+            g_pack[...] = pack(gat[it, pl.ds(plan.base[0] + cols, rank)])
+        here = pl.ds(p * cols, cols)
+        old = h_ref[here]
+        new = old * gat[it, pl.ds(plan.base[p], cols)] / dot_packed(old, g_pack[...])
+        h_ref[here] = new
+        if it == ITERS - 1:
+            h_store[p].start()
+        pair = jnp.concatenate(split(new), axis=1)
+        turned = jnp.concatenate(split(new.T), axis=0)
+        part_f = gram_of(turned, pair)
+        tail = pl.ds(units, rank)
+        q_own[it, tail] = part_f if p == 0 else q_own[it, tail] + part_f
+        crossing = []
+        if p == PARTS - 1:
+            crossing.append(q_copy(it, 0, units, rank))
+            crossing[0].start()
+        for b in range(units // block):
+            rows = pl.ds(b * block, block)
+            both = dot(a_high[p, rows], pair)
+            value = both[:, :rank] + (both[:, rank:] + dot(a_low[p, rows], pair[:, :rank]))
+            q_own[it, rows] = value if p == 0 else q_own[it, rows] + value
+            if p == PARTS - 1:
+                crossing.append(q_copy(it, b + 1, b * block, block))
+                crossing[-1].start()
+        return crossing
+
     w_ref[...] = w_in[...]
-    h_ref[...] = h_in[...]
     turned = w_in[...].T
     wt[:rank], wt[rank:] = split(turned)
+    h_store = [
+        pltpu.make_async_copy(
+            h_ref.at[pl.ds(p * cols, cols)], h_out.at[pl.ds(p * cols, cols)], load_sem.at[p]
+        )
+        for p in range(PARTS)
+    ]
 
     for it in range(ITERS):
-        sent = []
+        sent = {}
         for p in range(PARTS):
-            if p == 0:
-                acc[it, pl.ds(plan.base[0] + cols, rank)] = jnp.dot(
-                    w_ref[...].T, w_ref[...], precision=HI, preferred_element_type=jnp.float32
-                )
-            if plan.rows[p] > plan.used[p]:
-                spare = plan.rows[p] - plan.used[p]
-                acc[it, pl.ds(plan.base[p] + plan.used[p], spare)] = jnp.zeros(
-                    (spare, rank), jnp.float32
-                )
-            if it == 0:
-                loads[p].wait()
-                a_high[p], a_low[p] = split(a_f32[p])
-            both = dot(wt[...], a_high[p])
-            product = both[:rank] + (both[rank:] + dot(wt[:rank], a_low[p]))
-            acc[it, pl.ds(plan.base[p], cols)] = product.T
-            copies = rs_copies(it, p, 0)
-            start_all(copies)
-            sent.append(copies)
-
-        for t in range(3):
-            for p in range(PARTS):
-                size = sizes[p][t + 1]
-                mine = rows_at(offs[p][t + 1], size)
-                n = plan.dims[plan.orders[p][t]]
-                for copy in sent[p]:
-                    copy.wait()
-                value = acc[it, mine]
-                for k in range(1, n):
-                    value = value + rsr[it, pl.ds(plan.slot[p, t, k], size)]
-                if t < 2:
-                    acc[it, mine] = value
-                    sent[p] = rs_copies(it, p, t + 1)
-                else:
-                    gat[it, mine] = value
-                    sent[p] = ag_copies(it, p, 2)
-                start_all(sent[p])
-
-        for t in (2, 1, 0):
-            for p in range(PARTS):
-                for copy in sent[p]:
-                    copy.wait()
-                if t > 0:
-                    sent[p] = ag_copies(it, p, t - 1)
-                    start_all(sent[p])
-                    continue
-                here = pl.ds(p * cols, cols)
-                old = h_ref[here]
-                gram = gat[it, pl.ds(plan.base[0] + cols, rank)]
-                new = old * gat[it, pl.ds(plan.base[p], cols)] / jnp.dot(
-                    old, gram, precision=HI, preferred_element_type=jnp.float32
-                )
-                h_ref[here] = new
-                part_f = jnp.dot(
-                    new.T, new, precision=HI, preferred_element_type=jnp.float32
-                )
-                tail = pl.ds(units, rank)
-                q_own[it, tail] = part_f if p == 0 else q_own[it, tail] + part_f
-                crossing = []
-                if p == PARTS - 1:
-                    crossing.append(q_copy(it, 0, units, rank))
-                    crossing[0].start()
-                high, low = split(new)
-                pair = jnp.concatenate([high, low], axis=1)
-                for b in range(units // block):
-                    rows = pl.ds(b * block, block)
-                    both = dot(a_high[p, rows], pair)
-                    value = both[:, :rank] + (both[:, rank:] + dot(a_low[p, rows], high))
-                    q_own[it, rows] = value if p == 0 else q_own[it, rows] + value
-                    if p == PARTS - 1:
-                        crossing.append(q_copy(it, b + 1, b * block, block))
-                        crossing[-1].start()
+            products(it, p, sent)
+        if it == 0:
+            h_load.wait()
+        crossing = []
+        for p, stage in EVENTS:
+            advance(it, p, stage, sent)
+            if stage == 5:
+                crossing = update_sample(it, p, h_store)
 
         crossing[0].wait()
-        f_sum[...] = q_own[it, pl.ds(units, rank)] + q_peer[it, pl.ds(units, rank)]
+        f_pack[...] = pack(q_own[it, pl.ds(units, rank)] + q_peer[it, pl.ds(units, rank)])
         for b in range(units // block):
             rows = pl.ds(b * block, block)
             crossing[b + 1].wait()
             old = w_ref[rows]
-            new = old * (q_own[it, rows] + q_peer[it, rows]) / jnp.dot(
-                old, f_sum[...], precision=HI, preferred_element_type=jnp.float32
-            )
+            new = old * (q_own[it, rows] + q_peer[it, rows]) / dot_packed(old, f_pack[...])
             w_ref[rows] = new
             if it < ITERS - 1:
                 wt[:rank, rows], wt[rank:, rows] = split(new.T)
+    for store in h_store:
+        store.wait()
+
+
+def carry(w_ref, h_ref, w_out, h_out, sems):
+    copies = [
+        pltpu.make_async_copy(w_ref, w_out, sems.at[0]),
+        pltpu.make_async_copy(h_ref, h_out, sems.at[1]),
+    ]
+    for copy in copies:
+        copy.start()
+    for copy in copies:
+        copy.wait()
 
 
 def shards(unit, abundance, unitig_factor, sample_factor):
@@ -259,14 +312,16 @@
     vmem = pl.BlockSpec(memory_space=pltpu.VMEM)
     blocks = units // 256 + 1
     flops = 4 * 3 * 2 * units * samples * rank
-    return pl.pallas_call(
+    hbm = pl.BlockSpec(memory_space=pl.ANY)
+    results = (
+        jax.ShapeDtypeStruct((units, rank), f32),
+        jax.ShapeDtypeStruct((samples, rank), f32),
+    )
+    w_new, h_new = pl.pallas_call(
         functools.partial(kernel, plan),
-        out_shape=(
-            jax.ShapeDtypeStruct((units, rank), f32),
-            jax.ShapeDtypeStruct((samples, rank), f32),
-        ),
-        in_specs=[pl.BlockSpec(memory_space=pl.ANY), vmem, vmem],
-        out_specs=(vmem, vmem),
+        out_shape=results,
+        in_specs=[hbm, vmem, hbm],
+        out_specs=(vmem, hbm),
         scratch_shapes=[
             pltpu.VMEM((PARTS, units, cols), f32),
             pltpu.VMEM((PARTS, units, cols), BF),
@@ -277,8 +332,11 @@
             pltpu.VMEM((ITERS, plan.recv_rows, rank), f32),
             pltpu.VMEM((ITERS, units + rank, rank), f32),
             pltpu.VMEM((ITERS, units + rank, rank), f32),
-            pltpu.VMEM((rank, rank), f32),
+            pltpu.VMEM((2 * rank, 2 * rank), BF),
+            pltpu.VMEM((2 * rank, 2 * rank), BF),
+            pltpu.VMEM((samples, rank), f32),
             pltpu.SemaphoreType.DMA((PARTS,)),
+            pltpu.SemaphoreType.DMA,
             pltpu.SemaphoreType.DMA((ITERS, plan.sems)),
             pltpu.SemaphoreType.DMA((ITERS, plan.sems)),
             pltpu.SemaphoreType.DMA((ITERS, plan.sems)),
@@ -293,6 +351,13 @@
             flops=flops, bytes_accessed=4 * units * samples, transcendentals=0
         ),
     )(abundance, unitig_factor, sample_factor)
+    return pl.pallas_call(
+        carry,
+        out_shape=results,
+        in_specs=[hbm, hbm],
+        out_specs=(hbm, hbm),
+        scratch_shapes=[pltpu.SemaphoreType.DMA((2,))],
+    )(w_new, h_new)
 
 
 def solution(mesh):

time: 95 us -> 139 us (1.46)
  Pallas kernels: 90 us -> 138 us
  local copies, waits for them, and re-layouts: 4.13 us -> 0 us
    pallas_call x1 -> x2, Pallas kernels: 90 us -> 138 us  [the longest x1 89.4 us: shards(): pl.pallas_call(functools.partial(kernel, plan), out_shape=results, in_spe...]
    unnamed x2 -> x0, local copies, waits for them, and re-layouts: 4.13 us -> none
where the time goes in v2:
time: 139 us
  Pallas kernels  138 us (99%)
    pallas_call x1, Pallas kernels, shards(): pl.pallas_call(functools.partial(kernel, plan), out_shape=results, in_spe...  89.4 us
    pallas_call x1, Pallas kernels, shards(): pl.pallas_call(carry, out_shape=results, in_specs=[hbm, hbm], out_specs=(...  48.8 us

profile of v2, /device:TPU:0, one launch (start us, length us, event | category | flops | bytes accessed | tf_op | source)
XLA Modules:
  0.0 138.8 jit_solution(18282861565327335187)
XLA Ops:
  0.6 89.4 %shard_map.50 = (f32[1024,128]{1,0:T(8,128)}, f32[2048,128]{1,0:T(8,128)}) custom-call(f32[1024,2048]{1,0:T(8,128)} %a_hbm.1, f32[1024,128]{1,0:T(8,128)} %w_in.1, f32[2048,128]{1,0:T(8,128)} %h_in.1), custom_call_target="tpu_custom_call" | custom-call | flops 6442450944 | bytes 8388608 | tf_op jit(solution)/shard_map/pallas_call | solution.py:320
  90.1 48.8 %shard_map.51 = (f32[1024,128]{1,0:T(8,128)}, f32[2048,128]{1,0:T(8,128)}) custom-call(f32[1024,128]{1,0:T(8,128)} %get-tuple-element.4.w_ref, f32[2048,128]{1,0:T(8,128)} %get-tuple-element.5.h_ref), custom_call_target="tpu_custom_call" | custom-call | tf_op jit(solution)/shard_map/pallas_call | solution.py:354

commit v3 on v2

--- a/solution.py
+++ b/solution.py
@@ -91,7 +91,7 @@
 
 def kernel(
     plan, a_hbm, w_in, h_in, w_ref, h_out,
-    a_f32, a_high, a_low, wt, acc, gat, rsr, q_own, q_peer, g_pack, f_pack, h_ref,
+    a_f32, a_high, a_low, wt, acc, gat, rsr, q_own, q_peer, g_pack, f_pack, h_ref, pair_ref,
     load_sem, h_sem, rs_send, rs_recv, ag_send, ag_recv, q_send, q_recv,
 ):
     units, rank = w_in.shape
@@ -197,14 +197,19 @@
             acc[it, pl.ds(plan.base[p] + plan.used[p], spare)] = jnp.zeros(
                 (spare, rank), jnp.float32
             )
-        if it == 0:
+
+        @pl.when(it == 0)
+        def _():
             loads[p].wait()
-            a_high[p], a_low[p] = split(a_f32[p])
+
+            @pl.loop(0, units // block)
+            def _(b):
+                rows = pl.ds(pl.multiple_of(b * block, block), block)
+                a_high[p, rows], a_low[p, rows] = split(a_f32[p, rows])
+
         both = dot(wt[...], a_high[p])
         product = both[:rank] + (both[rank:] + dot(wt[:rank], a_low[p]))
         acc[it, pl.ds(plan.base[p], cols)] = product.T
-        if it == 0 and p == 0:
-            pl.semaphore_wait(barrier, greeted)
         sent[p] = rs_copies(it, p, 0)
         start_all(sent[p])
 
@@ -235,26 +240,29 @@
         old = h_ref[here]
         new = old * gat[it, pl.ds(plan.base[p], cols)] / dot_packed(old, g_pack[...])
         h_ref[here] = new
-        if it == ITERS - 1:
+
+        @pl.when(it == ITERS - 1)
+        def _():
             h_store[p].start()
+
         pair = jnp.concatenate(split(new), axis=1)
         turned = jnp.concatenate(split(new.T), axis=0)
         part_f = gram_of(turned, pair)
         tail = pl.ds(units, rank)
         q_own[it, tail] = part_f if p == 0 else q_own[it, tail] + part_f
-        crossing = []
         if p == PARTS - 1:
-            crossing.append(q_copy(it, 0, units, rank))
-            crossing[0].start()
-        for b in range(units // block):
-            rows = pl.ds(b * block, block)
-            both = dot(a_high[p, rows], pair)
-            value = both[:, :rank] + (both[:, rank:] + dot(a_low[p, rows], pair[:, :rank]))
+            q_copy(it, units // block, units, rank).start()
+        pair_ref[...] = pair
+
+        @pl.loop(0, units // block)
+        def _(b):
+            first = pl.multiple_of(b * block, block)
+            rows = pl.ds(first, block)
+            both = dot(a_high[p, rows], pair_ref[...])
+            value = both[:, :rank] + (both[:, rank:] + dot(a_low[p, rows], pair_ref[:, :rank]))
             q_own[it, rows] = value if p == 0 else q_own[it, rows] + value
             if p == PARTS - 1:
-                crossing.append(q_copy(it, b + 1, b * block, block))
-                crossing[-1].start()
-        return crossing
+                q_copy(it, b, first, block).start()
 
     w_ref[...] = w_in[...]
     turned = w_in[...].T
@@ -266,28 +274,32 @@
         for p in range(PARTS)
     ]
 
-    for it in range(ITERS):
+    h_load.wait()
+    pl.semaphore_wait(barrier, greeted)
+
+    @pl.loop(0, ITERS)
+    def _(it):
         sent = {}
         for p in range(PARTS):
             products(it, p, sent)
-        if it == 0:
-            h_load.wait()
-        crossing = []
         for p, stage in EVENTS:
             advance(it, p, stage, sent)
             if stage == 5:
-                crossing = update_sample(it, p, h_store)
-
-        crossing[0].wait()
+                update_sample(it, p, h_store)
+
+        q_copy(it, units // block, units, rank).wait()
         f_pack[...] = pack(q_own[it, pl.ds(units, rank)] + q_peer[it, pl.ds(units, rank)])
-        for b in range(units // block):
-            rows = pl.ds(b * block, block)
-            crossing[b + 1].wait()
+
+        @pl.loop(0, units // block)
+        def _(b):
+            first = pl.multiple_of(b * block, block)
+            rows = pl.ds(first, block)
+            q_copy(it, b, first, block).wait()
             old = w_ref[rows]
             new = old * (q_own[it, rows] + q_peer[it, rows]) / dot_packed(old, f_pack[...])
             w_ref[rows] = new
-            if it < ITERS - 1:
-                wt[:rank, rows], wt[rank:, rows] = split(new.T)
+            wt[:rank, rows], wt[rank:, rows] = split(new.T)
+
     for store in h_store:
         store.wait()
 
@@ -335,6 +347,7 @@
             pltpu.VMEM((2 * rank, 2 * rank), BF),
             pltpu.VMEM((2 * rank, 2 * rank), BF),
             pltpu.VMEM((samples, rank), f32),
+            pltpu.VMEM((cols, 2 * rank), BF),
             pltpu.SemaphoreType.DMA((PARTS,)),
             pltpu.SemaphoreType.DMA,
             pltpu.SemaphoreType.DMA((ITERS, plan.sems)),
@@ -354,7 +367,7 @@
     return pl.pallas_call(
         carry,
         out_shape=results,
-        in_specs=[hbm, hbm],
+        in_specs=[vmem, vmem],
         out_specs=(hbm, hbm),
         scratch_shapes=[pltpu.SemaphoreType.DMA((2,))],
     )(w_new, h_new)

time: 139 us -> 99.3 us (0.71)
  Pallas kernels: 138 us -> 98.5 us
    pallas_call x1, Pallas kernels: 48.8 us -> 2.55 us  [shards(): pl.pallas_call(carry, out_shape=results, in_specs=[vmem, vmem], out_specs...]
    pallas_call x1, Pallas kernels: 89.4 us -> 95.9 us  [shards(): pl.pallas_call(functools.partial(kernel, plan), out_shape=results, in_spe...]
where the time goes in v3:
time: 99.3 us; the launch traced here: 99.1 us
  Pallas kernels  98.5 us (99%)
    pallas_call x1, Pallas kernels, shards(): pl.pallas_call(functools.partial(kernel, plan), out_shape=results, in_spe...  95.9 us
    pallas_call x1, Pallas kernels, shards(): pl.pallas_call(carry, out_shape=results, in_specs=[vmem, vmem], out_specs...  2.55 us

profile of v3, /device:TPU:0, one launch (start us, length us, event | category | flops | bytes accessed | tf_op | source)
XLA Modules:
  0.0 99.1 jit_solution(16697330613008160149)
XLA Ops:
  0.6 95.9 %shard_map.50 = (f32[1024,128]{1,0:T(8,128)}, f32[2048,128]{1,0:T(8,128)}) custom-call(f32[1024,2048]{1,0:T(8,128)} %a_hbm.1, f32[1024,128]{1,0:T(8,128)} %w_in.1, f32[2048,128]{1,0:T(8,128)} %h_in.1), custom_call_target="tpu_custom_call" | custom-call | flops 6442450944 | bytes 8388608 | tf_op jit(solution)/shard_map/pallas_call | solution.py:332
  96.5 2.5 %shard_map.51 = (f32[1024,128]{1,0:T(8,128)}, f32[2048,128]{1,0:T(8,128)}) custom-call(f32[1024,128]{1,0:T(8,128)} %get-tuple-element.4.w_ref, f32[2048,128]{1,0:T(8,128)} %get-tuple-element.5.h_ref), custom_call_target="tpu_custom_call" | custom-call | tf_op jit(solution)/shard_map/pallas_call | solution.py:367

commit v4 on v2

--- a/solution.py
+++ b/solution.py
@@ -8,7 +8,10 @@
 from jax.sharding import PartitionSpec as P
 
 ITERS = 2
-PARTS = 4
+PARTS = 5
+SHARES = (3, 3, 4, 3, 3)
+ORDERS = ((2, 0, 1), (0, 1, 2), (1, 0, 2), (0, 1, 2), (1, 0, 2))
+LEAD = 1
 MESH = pl.DeviceIdType.MESH
 BF = jnp.bfloat16
 
@@ -26,10 +29,11 @@
         self.dims = chip_dims(unit)
         x, y, _ = self.dims
         self.strides = (1, x, x * y)
-        self.orders = [(0, 1, 2) if p % 2 == 0 else (1, 0, 2) for p in range(PARTS)]
-        self.cols = samples // PARTS
+        self.orders = ORDERS
+        self.cols = [samples // 16 * share for share in SHARES]
+        self.first = [sum(self.cols[:p]) for p in range(PARTS)]
         granule = 8 * unit
-        self.used = [self.cols + (rank if p == 0 else 0) for p in range(PARTS)]
+        self.used = [self.cols[p] + (rank if p == LEAD else 0) for p in range(PARTS)]
         self.rows = [-(-used // granule) * granule for used in self.used]
         self.base = [sum(self.rows[:p]) for p in range(PARTS)]
         self.total = sum(self.rows)
@@ -83,10 +87,11 @@
 
 
 EVENTS = (
-    (0, 0), (1, 0), (0, 1), (1, 1), (2, 0), (3, 0), (0, 2), (1, 2), (2, 1), (3, 1),
-    (0, 3), (1, 3), (2, 2), (3, 2), (0, 4), (1, 4), (0, 5), (2, 3), (3, 3), (1, 5),
-    (2, 4), (3, 4), (2, 5), (3, 5),
+    (1, 0), (2, 0), (3, 0), (0, 0), (4, 0), (1, 1), (2, 1), (0, 1), (3, 1), (4, 1),
+    (1, 2), (2, 2), (0, 2), (3, 2), (4, 2), (1, 3), (0, 3), (2, 3), (0, 4), (3, 3),
+    (4, 3), (1, 4), (2, 4), (3, 4), (4, 4), (1, 5), (2, 5), (0, 5), (3, 5), (4, 5),
 )
+LAST = EVENTS[-1][0]
 
 
 def kernel(
@@ -95,7 +100,6 @@
     load_sem, h_sem, rs_send, rs_recv, ag_send, ag_recv, q_send, q_recv,
 ):
     units, rank = w_in.shape
-    cols = plan.cols
     me = lax.axis_index("unit")
     core = lax.axis_index("samp")
     place = [lax.rem(me // plan.strides[d], plan.dims[d]) for d in range(3)]
@@ -103,7 +107,9 @@
 
     loads = [
         pltpu.make_async_copy(
-            a_hbm.at[:, pl.ds(p * cols, cols)], a_f32.at[p], load_sem.at[p]
+            a_hbm.at[:, pl.ds(plan.first[p], plan.cols[p])],
+            a_f32.at[:, pl.ds(plan.first[p], plan.cols[p])],
+            load_sem.at[p],
         )
         for p in range(PARTS)
     ]
@@ -188,8 +194,9 @@
             copy.start()
 
     def products(it, p, sent):
-        if p == 0:
-            acc[it, pl.ds(plan.base[0] + cols, rank)] = gram_of(
+        here = pl.ds(plan.first[p], plan.cols[p])
+        if p == LEAD:
+            acc[it, pl.ds(plan.base[p] + plan.cols[p], rank)] = gram_of(
                 wt[...], jnp.concatenate(split(w_ref[...]), axis=1)
             )
         if plan.rows[p] > plan.used[p]:
@@ -199,10 +206,10 @@
             )
         if it == 0:
             loads[p].wait()
-            a_high[p], a_low[p] = split(a_f32[p])
-        both = dot(wt[...], a_high[p])
-        product = both[:rank] + (both[rank:] + dot(wt[:rank], a_low[p]))
-        acc[it, pl.ds(plan.base[p], cols)] = product.T
+            a_high[:, here], a_low[:, here] = split(a_f32[:, here])
+        both = dot(wt[...], a_high[:, here])
+        product = both[:rank] + (both[rank:] + dot(wt[:rank], a_low[:, here]))
+        acc[it, pl.ds(plan.base[p], plan.cols[p])] = product.T
         if it == 0 and p == 0:
             pl.semaphore_wait(barrier, greeted)
         sent[p] = rs_copies(it, p, 0)
@@ -229,11 +236,11 @@
             start_all(sent[p])
 
     def update_sample(it, p, h_store):
-        if p == 0:
-            g_pack[...] = pack(gat[it, pl.ds(plan.base[0] + cols, rank)])
-        here = pl.ds(p * cols, cols)
+        if p == LEAD:
+            g_pack[...] = pack(gat[it, pl.ds(plan.base[p] + plan.cols[p], rank)])
+        here = pl.ds(plan.first[p], plan.cols[p])
         old = h_ref[here]
-        new = old * gat[it, pl.ds(plan.base[p], cols)] / dot_packed(old, g_pack[...])
+        new = old * gat[it, pl.ds(plan.base[p], plan.cols[p])] / dot_packed(old, g_pack[...])
         h_ref[here] = new
         if it == ITERS - 1:
             h_store[p].start()
@@ -241,17 +248,17 @@
         turned = jnp.concatenate(split(new.T), axis=0)
         part_f = gram_of(turned, pair)
         tail = pl.ds(units, rank)
-        q_own[it, tail] = part_f if p == 0 else q_own[it, tail] + part_f
+        q_own[it, tail] = part_f if p == LEAD else q_own[it, tail] + part_f
         crossing = []
-        if p == PARTS - 1:
+        if p == LAST:
             crossing.append(q_copy(it, 0, units, rank))
             crossing[0].start()
         for b in range(units // block):
             rows = pl.ds(b * block, block)
-            both = dot(a_high[p, rows], pair)
-            value = both[:, :rank] + (both[:, rank:] + dot(a_low[p, rows], pair[:, :rank]))
-            q_own[it, rows] = value if p == 0 else q_own[it, rows] + value
-            if p == PARTS - 1:
+            both = dot(a_high[rows, here], pair)
+            value = both[:, :rank] + (both[:, rank:] + dot(a_low[rows, here], pair[:, :rank]))
+            q_own[it, rows] = value if p == LEAD else q_own[it, rows] + value
+            if p == LAST:
                 crossing.append(q_copy(it, b + 1, b * block, block))
                 crossing[-1].start()
         return crossing
@@ -261,7 +268,9 @@
     wt[:rank], wt[rank:] = split(turned)
     h_store = [
         pltpu.make_async_copy(
-            h_ref.at[pl.ds(p * cols, cols)], h_out.at[pl.ds(p * cols, cols)], load_sem.at[p]
+            h_ref.at[pl.ds(plan.first[p], plan.cols[p])],
+            h_out.at[pl.ds(plan.first[p], plan.cols[p])],
+            load_sem.at[p],
         )
         for p in range(PARTS)
     ]
@@ -307,7 +316,6 @@
     units, samples = abundance.shape
     rank = unitig_factor.shape[1]
     plan = Plan(unit, samples, rank)
-    cols = plan.cols
     f32 = jnp.float32
     vmem = pl.BlockSpec(memory_space=pltpu.VMEM)
     blocks = units // 256 + 1
@@ -323,9 +331,9 @@
         in_specs=[hbm, vmem, hbm],
         out_specs=(vmem, hbm),
         scratch_shapes=[
-            pltpu.VMEM((PARTS, units, cols), f32),
-            pltpu.VMEM((PARTS, units, cols), BF),
-            pltpu.VMEM((PARTS, units, cols), BF),
+            pltpu.VMEM((units, samples), f32),
+            pltpu.VMEM((units, samples), BF),
+            pltpu.VMEM((units, samples), BF),
             pltpu.VMEM((2 * rank, units), BF),
             pltpu.VMEM((ITERS, plan.total, rank), f32),
             pltpu.VMEM((ITERS, plan.total, rank), f32),
@@ -354,7 +362,7 @@
     return pl.pallas_call(
         carry,
         out_shape=results,
-        in_specs=[hbm, hbm],
+        in_specs=[vmem, vmem],
         out_specs=(hbm, hbm),
         scratch_shapes=[pltpu.SemaphoreType.DMA((2,))],
     )(w_new, h_new)

time: 139 us -> 84 us (0.60)
  Pallas kernels: 138 us -> 82.9 us
    pallas_call x1, Pallas kernels: 48.8 us -> 2.55 us  [shards(): pl.pallas_call(carry, out_shape=results, in_specs=[vmem, vmem], out_specs...]
    pallas_call x1, Pallas kernels: 89.4 us -> 80.3 us  [shards(): pl.pallas_call(functools.partial(kernel, plan), out_shape=results, in_spe...]
where the time goes in v4:
time: 84 us; the launch traced here: 83.7 us
  Pallas kernels  82.9 us (99%)
    pallas_call x1, Pallas kernels, shards(): pl.pallas_call(functools.partial(kernel, plan), out_shape=results, in_spe...  80.3 us
    pallas_call x1, Pallas kernels, shards(): pl.pallas_call(carry, out_shape=results, in_specs=[vmem, vmem], out_specs...  2.55 us

profile of v4, /device:TPU:0, one launch (start us, length us, event | category | flops | bytes accessed | tf_op | source)
XLA Modules:
  0.0 83.7 jit_solution(14705265186138038301)
XLA Ops:
  0.6 80.3 %shard_map.50 = (f32[1024,128]{1,0:T(8,128)}, f32[2048,128]{1,0:T(8,128)}) custom-call(f32[1024,2048]{1,0:T(8,128)} %a_hbm.1, f32[1024,128]{1,0:T(8,128)} %w_in.1, f32[2048,128]{1,0:T(8,128)} %h_in.1), custom_call_target="tpu_custom_call" | custom-call | flops 6442450944 | bytes 8388608 | tf_op jit(solution)/shard_map/pallas_call | solution.py:328
  81.0 2.5 %shard_map.51 = (f32[1024,128]{1,0:T(8,128)}, f32[2048,128]{1,0:T(8,128)}) custom-call(f32[1024,128]{1,0:T(8,128)} %get-tuple-element.4.w_ref, f32[2048,128]{1,0:T(8,128)} %get-tuple-element.5.h_ref), custom_call_target="tpu_custom_call" | custom-call | tf_op jit(solution)/shard_map/pallas_call | solution.py:362

commit v5 on v4

--- a/solution.py
+++ b/solution.py
@@ -9,8 +9,8 @@
 
 ITERS = 2
 PARTS = 5
-SHARES = (3, 3, 4, 3, 3)
-ORDERS = ((2, 0, 1), (0, 1, 2), (1, 0, 2), (0, 1, 2), (1, 0, 2))
+SHARES = (2, 4, 4, 4, 2)
+ORDERS = ((2, 0, 1), (0, 1, 2), (1, 0, 2), (1, 0, 2), (0, 1, 2))
 LEAD = 1
 MESH = pl.DeviceIdType.MESH
 BF = jnp.bfloat16
@@ -87,9 +87,9 @@
 
 
 EVENTS = (
-    (1, 0), (2, 0), (3, 0), (0, 0), (4, 0), (1, 1), (2, 1), (0, 1), (3, 1), (4, 1),
-    (1, 2), (2, 2), (0, 2), (3, 2), (4, 2), (1, 3), (0, 3), (2, 3), (0, 4), (3, 3),
-    (4, 3), (1, 4), (2, 4), (3, 4), (4, 4), (1, 5), (2, 5), (0, 5), (3, 5), (4, 5),
+    (1, 0), (0, 0), (2, 0), (4, 0), (3, 0), (1, 1), (2, 1), (0, 1), (4, 1), (3, 1),
+    (1, 2), (2, 2), (0, 2), (4, 2), (3, 2), (1, 3), (0, 3), (2, 3), (0, 4), (4, 3),
+    (3, 3), (1, 4), (2, 4), (4, 4), (3, 4), (1, 5), (2, 5), (0, 5), (4, 5), (3, 5),
 )
 LAST = EVENTS[-1][0]
 
@@ -113,8 +113,8 @@
         )
         for p in range(PARTS)
     ]
-    for load in loads:
-        load.start()
+    for p in (0, 1, 2, 4, 3):
+        loads[p].start()
     h_load = pltpu.make_async_copy(h_in, h_ref, h_sem)
     h_load.start()
 
@@ -277,7 +277,7 @@
 
     for it in range(ITERS):
         sent = {}
-        for p in range(PARTS):
+        for p in (0, 1, 2, 4, 3):
             products(it, p, sent)
         if it == 0:
             h_load.wait()

time: 84 us -> 86.4 us (1.029)
  Pallas kernels: 82.9 us -> 85.4 us
    pallas_call x1, Pallas kernels: 80.3 us -> 82.9 us  [shards(): pl.pallas_call(functools.partial(kernel, plan), out_shape=results, in_spe...]
where the time goes in v5:
time: 86.4 us; the launch traced here: 86.2 us
  Pallas kernels  85.4 us (99%)
    pallas_call x1, Pallas kernels, shards(): pl.pallas_call(functools.partial(kernel, plan), out_shape=results, in_spe...  82.9 us
    pallas_call x1, Pallas kernels, shards(): pl.pallas_call(carry, out_shape=results, in_specs=[vmem, vmem], out_specs...  2.55 us

profile of v5, /device:TPU:0, one launch (start us, length us, event | category | flops | bytes accessed | tf_op | source)
XLA Modules:
  0.0 86.2 jit_solution(17931975631192172362)
XLA Ops:
  0.6 82.9 %shard_map.50 = (f32[1024,128]{1,0:T(8,128)}, f32[2048,128]{1,0:T(8,128)}) custom-call(f32[1024,2048]{1,0:T(8,128)} %a_hbm.1, f32[1024,128]{1,0:T(8,128)} %w_in.1, f32[2048,128]{1,0:T(8,128)} %h_in.1), custom_call_target="tpu_custom_call" | custom-call | flops 6442450944 | bytes 8388608 | tf_op jit(solution)/shard_map/pallas_call | solution.py:328
  83.5 2.5 %shard_map.51 = (f32[1024,128]{1,0:T(8,128)}, f32[2048,128]{1,0:T(8,128)}) custom-call(f32[1024,128]{1,0:T(8,128)} %get-tuple-element.4.w_ref, f32[2048,128]{1,0:T(8,128)} %get-tuple-element.5.h_ref), custom_call_target="tpu_custom_call" | custom-call | tf_op jit(solution)/shard_map/pallas_call | solution.py:362

commit v6 on v4

--- a/solution.py
+++ b/solution.py
@@ -8,9 +8,9 @@
 from jax.sharding import PartitionSpec as P
 
 ITERS = 2
-PARTS = 5
-SHARES = (3, 3, 4, 3, 3)
-ORDERS = ((2, 0, 1), (0, 1, 2), (1, 0, 2), (0, 1, 2), (1, 0, 2))
+PARTS = 4
+SHARES = (4, 4, 4, 4)
+ORDERS = ((2, 0, 1), (0, 1, 2), (1, 0, 2), (1, 0, 2))
 LEAD = 1
 MESH = pl.DeviceIdType.MESH
 BF = jnp.bfloat16
@@ -87,9 +87,9 @@
 
 
 EVENTS = (
-    (1, 0), (2, 0), (3, 0), (0, 0), (4, 0), (1, 1), (2, 1), (0, 1), (3, 1), (4, 1),
-    (1, 2), (2, 2), (0, 2), (3, 2), (4, 2), (1, 3), (0, 3), (2, 3), (0, 4), (3, 3),
-    (4, 3), (1, 4), (2, 4), (3, 4), (4, 4), (1, 5), (2, 5), (0, 5), (3, 5), (4, 5),
+    (1, 0), (2, 0), (0, 0), (3, 0), (1, 1), (2, 1), (0, 1), (3, 1),
+    (1, 2), (2, 2), (0, 2), (3, 2), (1, 3), (0, 3), (2, 3), (0, 4),
+    (3, 3), (1, 4), (2, 4), (3, 4), (1, 5), (2, 5), (0, 5), (3, 5),
 )
 LAST = EVENTS[-1][0]
 

time: 84 us -> 82.3 us (0.980)
  Pallas kernels: 82.9 us -> 81.5 us
    pallas_call x1, Pallas kernels: 80.3 us -> 78.9 us  [shards(): pl.pallas_call(functools.partial(kernel, plan), out_shape=results, in_spe...]
where the time goes in v6:
time: 82.3 us; the launch traced here: 82.1 us
  Pallas kernels  81.5 us (99%)
    pallas_call x1, Pallas kernels, shards(): pl.pallas_call(functools.partial(kernel, plan), out_shape=results, in_spe...  78.9 us
    pallas_call x1, Pallas kernels, shards(): pl.pallas_call(carry, out_shape=results, in_specs=[vmem, vmem], out_specs...  2.55 us

profile of v6, /device:TPU:0, one launch (start us, length us, event | category | flops | bytes accessed | tf_op | source)
XLA Modules:
  0.0 82.1 jit_solution(11465218029467212108)
XLA Ops:
  0.6 78.9 %shard_map.50 = (f32[1024,128]{1,0:T(8,128)}, f32[2048,128]{1,0:T(8,128)}) custom-call(f32[1024,2048]{1,0:T(8,128)} %a_hbm.1, f32[1024,128]{1,0:T(8,128)} %w_in.1, f32[2048,128]{1,0:T(8,128)} %h_in.1), custom_call_target="tpu_custom_call" | custom-call | flops 6442450944 | bytes 8388608 | tf_op jit(solution)/shard_map/pallas_call | solution.py:328
  79.6 2.5 %shard_map.51 = (f32[1024,128]{1,0:T(8,128)}, f32[2048,128]{1,0:T(8,128)}) custom-call(f32[1024,128]{1,0:T(8,128)} %get-tuple-element.4.w_ref, f32[2048,128]{1,0:T(8,128)} %get-tuple-element.5.h_ref), custom_call_target="tpu_custom_call" | custom-call | tf_op jit(solution)/shard_map/pallas_call | solution.py:362
